TPU v7x, 32 devices: a whole 2x2x4 slice. The times are simulated.
32 devices in a mesh: aux: 2 (over core), occ: 16 (over z, y, x).
Axes of the slice: x: 2, y: 2, z: 4, core: 2. Of those that a mesh axis runs over, the one named last changes fastest.
Arguments:
- factors: float32 [2048, 16, 512], P('aux', 'occ'), may hold values from -0.3 to 0.3
- eps_occ: float32 [16], P('occ'), may hold values from -2 to -0.3
- eps_virt: float32 [512], replicated, may hold values from 0.2 to 3
- pair_mask: int32 [16, 4], P('occ'), may hold values 0 or 1
Outputs:
- gradient: float32 [2048, 16, 512], P('aux', 'occ')
Inputs may be any that keep to these rules, and one draw needn't show every extreme that they name: `pair_mask`: 1 marks a surviving pair.
All inputs are finite; a program needn't handle non-finite values. No bound on the sum of `pair_mask` on one device may be relied on, other than what follows from the above.
Results may differ from a plain program's by a relative error of at most 0.0003.
Values sent between devices are 32-bit elements; how exact they have to be, the bound alone decides.
No kernel may reach another device: no remote copies, remote signals or barrier semaphores. Data moves between devices by JAX's collectives and lax.ppermute only.
A program may use at most 128 MiB of HBM per device.

v0:
```python
import dataclasses
import functools

import jax
import jax.numpy as jnp
from jax import lax
from jax.experimental import pallas as pl
from jax.experimental.pallas import tpu as pltpu
from jax.sharding import PartitionSpec as P

LANES = 128
SUBLANES = 8
PLANE = 4
CHUNKS = 4
VMEM_LIMIT = 60 * 1024 * 1024


def split(value):
    high = value.astype(jnp.bfloat16)
    low = (value - high.astype(jnp.float32)).astype(jnp.bfloat16)
    return high, low


def deep_left(value):
    high, low = split(value)
    return jnp.concatenate([high, low, high], axis=1)


def deep_right(value):
    high, low = split(value)
    return jnp.concatenate([high, high, low], axis=0)


def dot(left, right):
    numbers = (((1,), (0,)), ((), ()))
    return lax.dot_general(left, right, numbers, preferred_element_type=jnp.float32)


def rows_of(ref, start, count, width):
    lines = width // LANES
    columns = [ref[pl.ds(start * lines + at, count, stride=lines), :] for at in range(lines)]
    return jnp.concatenate(columns, axis=1)


def distinct(arrays):
    return list({id(array): array for array in arrays}.values())


class Copies:
    def __init__(self, semaphores):
        self.semaphores = semaphores
        self.used = 0

    def start(self, source, target):
        copy = pltpu.make_async_copy(source, target, self.semaphores.at[self.used])
        self.used += 1
        copy.start()
        return copy

    def start_piece(self, piece, ref_of, flags, count, target):
        made = []
        for array, base in piece.places:
            source = ref_of[id(array)].at[pl.ds(base, count)]
            made.append(pltpu.make_async_copy(source, target, self.semaphores.at[self.used]))
        self.used += 1
        if len(made) == 1:
            made[0].start()
        else:
            pl.when(flags[piece.flag] > 0)(made[0].start)
            pl.when(flags[piece.flag] <= 0)(made[1].start)
        return made[0]


@dataclasses.dataclass(frozen=True)
class Piece:
    places: tuple
    flag: int = 0


def call(kernel, smem, vmem, anywhere, outputs, out_space, scratch):
    spaces = [pltpu.SMEM] * len(smem) + [pltpu.VMEM] * len(vmem) + [pl.ANY] * len(anywhere)
    return pl.pallas_call(
        kernel,
        out_shape=outputs,
        in_specs=[pl.BlockSpec(memory_space=space) for space in spaces],
        out_specs=[pl.BlockSpec(memory_space=out_space)] * len(outputs),
        scratch_shapes=scratch,
        compiler_params=pltpu.CompilerParams(vmem_limit_bytes=VMEM_LIMIT),
        cost_estimate=pl.CostEstimate(flops=0, bytes_accessed=0, transcendentals=0),
    )(*smem, *vmem, *anywhere)


def prepare(own, rows, width):
    size = rows // CHUNKS
    cut = size * width // LANES

    def kernel(own_ref, high_ref, low_ref, integrals_ref, block_ref, semaphores):
        copies = Copies(semaphores)
        coming = [copies.start(own_ref.at[pl.ds(at * cut, cut)], block_ref.at[at]) for at in range(CHUNKS)]
        for at in range(CHUNKS):
            coming[at].wait()
            block = rows_of(block_ref.at[at], 0, size, width)
            high, low = split(block.T)
            high_ref[at] = high
            low_ref[at] = low
            value = dot(jnp.concatenate([high, low, high], axis=1), deep_right(block))
            integrals_ref[...] = integrals_ref[...] + value if at else value

    half = jax.ShapeDtypeStruct((CHUNKS, width, size), jnp.bfloat16)
    square = jax.ShapeDtypeStruct((width, width), jnp.float32)
    scratch = [pltpu.VMEM((CHUNKS, cut, LANES), jnp.float32), pltpu.SemaphoreType.DMA((CHUNKS,))]
    return call(kernel, [], [], [own], [half, half, square], pltpu.VMEM, scratch)


def arrays_of(pieces):
    return distinct([array for piece in pieces for array, _ in piece.places])


def integrate(turned, slots, first, flags, size, width, before=()):
    cut = size * width // LANES
    count = len(slots)
    pieces = [piece for slot in slots for piece in slot]
    arrays = arrays_of(pieces)
    numbers = [list(range(start, start + len(slot))) for slot, start in zip(slots, first)]
    needed = sorted({number for some in numbers for number in some})
    before = list(before)

    def kernel(flag_ref, *refs):
        given = iter(refs)
        high_ref, low_ref = next(given), next(given)
        before_refs = [next(given) for _ in before]
        ref_of = {id(array): next(given) for array in arrays}
        outs = [next(given) for _ in range(count)]
        turned_ref, block_ref, before_ref, semaphores = given
        copies = Copies(semaphores)
        coming, turning = [], {}

        def turn(number):
            if number not in turning:
                at = needed.index(number)
                turning[number] = [
                    copies.start(high_ref.at[number], turned_ref.at[at, 0]),
                    copies.start(low_ref.at[number], turned_ref.at[at, 1]),
                ]

        at = 0
        for slot in range(count):
            for number, piece in zip(numbers[slot], slots[slot]):
                turn(number)
                coming.append(copies.start_piece(piece, ref_of, flag_ref, cut, block_ref.at[at]))
                at += 1
        adding = [copies.start(ref, before_ref.at[slot]) for slot, ref in enumerate(before_refs)]
        at = 0
        for slot in range(count):
            for place, number in enumerate(numbers[slot]):
                for copy in turning.pop(number, []):
                    copy.wait()
                coming[at].wait()
                there = needed.index(number)
                high, low = turned_ref[there, 0], turned_ref[there, 1]
                left = jnp.concatenate([high, low, high], axis=1)
                value = dot(left, deep_right(rows_of(block_ref.at[at], 0, size, width)))
                outs[slot][...] = outs[slot][...] + value if place else value
                at += 1
            if before:
                adding[slot].wait()
                outs[slot][...] += before_ref[slot]

    out = [jax.ShapeDtypeStruct((width, width), jnp.float32)] * count
    scratch = [
        pltpu.VMEM((len(needed), 2, width, size), jnp.bfloat16),
        pltpu.VMEM((len(pieces), cut, LANES), jnp.float32),
        pltpu.VMEM((max(len(before), 1), width, width), jnp.float32),
        pltpu.SemaphoreType.DMA((2 * len(needed) + len(pieces) + len(before),)),
    ]
    return call(kernel, [flags], [], [*turned, *before, *arrays], out, pltpu.VMEM, scratch)


def contract(partials, slots, signs, energies, flags, eps_virt, size, before=None):
    count = len(slots)
    chunks = len(slots[0])
    virt = eps_virt.shape[1]
    width = partials[0][0].shape[0]
    occ_rows = width // virt
    lines = width // LANES
    cut = size * lines
    sums = [array for slot in partials for array in slot]
    pieces = [piece for slot in slots for piece in slot]
    arrays = arrays_of([*pieces, *energies])
    last = [before] if before is not None else []

    def kernel(*refs):
        given = iter(refs)
        sign_ref, flag_ref, virt_ref = next(given), next(given), next(given)
        sum_refs = [next(given) for _ in sums]
        before_refs = [next(given) for _ in last]
        ref_of = {id(array): next(given) for array in arrays}
        out_ref, energy_ref, sum_ref, block_ref, result_ref, right_ref, semaphores = given
        copies = Copies(semaphores)
        arriving = [
            copies.start_piece(piece, ref_of, flag_ref, SUBLANES, energy_ref.at[at])
            for at, piece in enumerate(energies)
        ]
        arriving += [copies.start(ref, sum_ref.at[at]) for at, ref in enumerate(sum_refs)]
        coming = [
            [
                copies.start_piece(slots[slot][at], ref_of, flag_ref, cut, block_ref.at[slot, at])
                for slot in range(count)
            ]
            for at in range(chunks)
        ]
        adding = [
            [copies.start(ref.at[pl.ds(at * cut, cut)], result_ref.at[at]) for ref in before_refs]
            for at in range(chunks)
        ]
        for copy in arriving:
            copy.wait()

        def line(at):
            virtual = virt_ref[...]
            energy = energy_ref[at]
            return jnp.concatenate([virtual - energy[:1, i : i + 1] for i in range(occ_rows)], axis=1)

        row = jnp.broadcast_to(line(0), (SUBLANES, width)).T[:, :1]
        at = 0
        for slot in range(count):
            total = sum_ref[at]
            for extra in range(1, len(partials[slot])):
                total = total + sum_ref[at + extra]
            at += len(partials[slot])
            amplitude = (sign_ref[slot] * total) / (row + line(slot + 1))
            right_ref[pl.ds(slot * 3 * width, 3 * width), :] = deep_right(amplitude.T)
        leaving = []
        for at in range(chunks):
            for copy in coming[at] + adding[at]:
                copy.wait()
            left = [deep_left(rows_of(block_ref.at[slot, at], 0, size, width)) for slot in range(count)]
            value = dot(jnp.concatenate(left, axis=1), right_ref[...])
            for column in range(lines):
                lanes = value[:, column * LANES : (column + 1) * LANES]
                where = pl.ds(column, size, stride=lines)
                if last:
                    lanes = lanes + result_ref[at, where, :]
                result_ref[at, where, :] = lanes
            leaving.append(copies.start(result_ref.at[at], out_ref.at[pl.ds(at * cut, cut)]))
        for copy in leaving:
            copy.wait()

    rows = chunks * size
    out = jax.ShapeDtypeStruct((rows * lines, LANES), jnp.float32)
    scratch = [
        pltpu.VMEM((len(energies), SUBLANES, LANES), jnp.float32),
        pltpu.VMEM((len(sums), width, width), jnp.float32),
        pltpu.VMEM((count, chunks, cut, LANES), jnp.float32),
        pltpu.VMEM((chunks, cut, LANES), jnp.float32),
        pltpu.VMEM((count * 3 * width, width), jnp.bfloat16),
        pltpu.SemaphoreType.DMA((len(energies) + len(sums) + len(pieces) + 2 * chunks,)),
    ]
    return call(kernel, [signs, flags], [eps_virt], [*sums, *last, *arrays], [out], pl.ANY, scratch)[0]


def after(block, *others):
    return lax.optimization_barrier((block, *others))[0]


def on_device(factors, eps_occ, eps_virt, pair_mask):
    rows, occ_rows, virt = factors.shape
    width = occ_rows * virt
    lines = width // LANES
    groups = lax.axis_size("occ")
    shares = lax.axis_size("aux")
    size = rows // CHUNKS
    cut = size * lines
    last = CHUNKS - 1
    group = lax.axis_index("occ")
    place = group % PLANE
    odd_x = place % 2 == 1
    odd_y = place // 2 == 1

    own = factors.reshape(rows * lines, LANES)
    energies = jnp.zeros((SUBLANES * LANES,), jnp.float32).at[:occ_rows].set(eps_occ)
    energies = energies.reshape(SUBLANES, LANES)

    def part(whole, at):
        return whole[at * cut : (at + 1) * cut]

    def within(block, moves):
        planes = range(0, groups, PLANE)
        return lax.ppermute(block, "occ", [(g + a, g + b) for g in planes for a, b in moves])

    def up(block):
        return lax.ppermute(block, "occ", [(g, g + PLANE) for g in range(groups - PLANE)])

    def totals(partial):
        if shares == 2:
            return [partial, lax.ppermute(partial, "aux", [(0, 1), (1, 0)])]
        return [lax.psum(partial, "aux")]

    def sign(offset):
        flag = lax.dynamic_index_in_dim(pair_mask[0], offset - 1, 0, keepdims=False)
        return jnp.where((group >= offset) & (flag > 0), -1.0, 0.0).astype(jnp.float32)

    sign_own = jnp.float32(-1.0)
    sign_z = sign(jnp.int32(PLANE))
    sign_x = sign(jnp.where(odd_x, 1, PLANE - 1))
    sign_y = sign(jnp.int32(PLANE // 2))
    sign_d = sign(jnp.where(odd_x, PLANE - 1, 1))

    first_sent = jnp.concatenate([part(own, 0), energies])
    flags = jnp.stack([odd_x, odd_y]).astype(jnp.int32)

    def add(partials, slots, signs, carriers, before=None):
        return contract(partials, slots, jnp.stack(signs), carriers, flags, eps_virt[None, :], size, before)

    from_z = [up(first_sent)]
    up_x = within(first_sent, [(0, 1), (2, 3), (1, 0)])
    up_y = within(first_sent, [(0, 2), (1, 3)])
    high, low, partial_own = prepare(own, rows, width)
    turned = (high, low)
    sums_own = totals(partial_own)
    swap_x, swap_y = [], []
    passed = [partial_own, up_x, up_y]
    for at in range(CHUNKS):
        came, mine, *_ = lax.optimization_barrier((from_z[at], own, *passed))
        if at < last:
            from_z.append(up(part(mine, at + 1)))
            up_part = part(mine, at + 1)
            if at == 0:
                up_part = jnp.concatenate([up_part, energies])
            swap_x.append(within(jnp.where(odd_x, came, up_part), [(0, 1), (1, 0), (2, 3), (3, 2)]))
            swap_y.append(within(jnp.where(odd_y, came, up_part), [(0, 2), (2, 0), (1, 3), (3, 1)]))
        else:
            swap_x.append(within(came, [(1, 0), (3, 2)]))
            swap_y.append(within(came, [(2, 0), (3, 1)]))
        passed = [swap_x[at], swap_y[at]]
        if at == 0:
            up_d = within(up_x, [(0, 2), (1, 3)])
        if at == 2:
            passed.append(up_d)

    middle = (place == 1) | (place == 2)
    half = CHUNKS // 2
    block = jnp.where(middle, jnp.concatenate(swap_x[:half]), jnp.concatenate(swap_y[:half]))
    block = after(block, swap_x[half], swap_y[half])
    cycle = within(block, [(0, 1), (1, 3), (3, 2), (2, 0)])
    swap_d = [(cycle, 0)] + [(cycle, at * cut + SUBLANES) for at in range(1, half)]
    for at in range(half, CHUNKS):
        moves = [(0, 1), (1, 0), (2, 3), (3, 2)] if at < last else [(0, 1), (1, 0)]
        swap_d.append((within(swap_y[at], moves), 0))

    def pieces_of(first, swaps, flag, base):
        places = [(array, start + base) for array, start in [(first, 0), *swaps]]
        return [Piece((places[at], places[at + 1]), flag) for at in range(CHUNKS)]

    swap_x = [(block, 0) for block in swap_x]
    swap_y = [(block, 0) for block in swap_y]

    def whole(array, base):
        return Piece(((array, base),))

    slot_own = [whole(own, at * cut) for at in range(CHUNKS)]
    slot_z = [whole(block, 0) for block in from_z]
    slot_x = pieces_of(up_x, swap_x, 0, 0)
    slot_y = pieces_of(up_y, swap_y, 1, 0)
    slot_d = pieces_of(up_d, swap_d, 1, 0)
    eps_x = pieces_of(up_x, swap_x, 0, cut)[0]
    eps_y = pieces_of(up_y, swap_y, 1, cut)[0]
    eps_d = pieces_of(up_d, swap_d, 1, cut)[0]

    (partial_z,) = integrate(after(turned, block), [slot_z], [0], flags, size, width)
    gradient = add(
        [sums_own, totals(partial_z)], [slot_own, slot_z], [sign_own, sign_z],
        [whole(first_sent, cut), whole(first_sent, cut), whole(from_z[0], cut)],
    )
    partial_x, partial_y = integrate(turned, [slot_x, slot_y], [0, 0], flags, size, width)
    gradient = add(
        [totals(partial_x), totals(partial_y)], [slot_x, slot_y], [sign_x, sign_y],
        [whole(first_sent, cut), eps_x, eps_y], gradient,
    )
    turned = after(turned, gradient)
    partial_d = integrate(turned, [slot_d[:last]], [0], flags, size, width)
    (partial_d,) = integrate(turned, [slot_d[last:]], [last], flags, size, width, partial_d)
    gradient = add([totals(partial_d)], [slot_d], [sign_d], [whole(first_sent, cut), eps_d], gradient)
    return gradient.reshape(rows, occ_rows, virt)


def solution(mesh):
    if mesh.shape["occ"] % PLANE:
        raise ValueError("incomplete plane")
    in_specs = (P("aux", "occ", None), P("occ"), P(), P("occ", None))
    out_specs = P("aux", "occ", None)
    return jax.shard_map(
        on_device, mesh=mesh, in_specs=in_specs, out_specs=out_specs, check_vma=False
    )
```

profile of v0, /device:TPU:0, one launch (start us, length us, event | category | flops | bytes accessed | tf_op | source)
XLA Modules:
  0.0 147.7 jit_solution(5709845709199597239)
XLA Ops:
  1.1 4.8 %collective-permute-start = (f32[1032,128]{1,0:T(8,128)S(1)}, f32[1032,128]{1,0:T(8,128)}, u32[]{:S(2)}, u32[]{:S(2)}) collective-permute-start(f32[1032,128]{1,0:T(8,128)S(1)} %pad_maximum_fusion.1.refs_12_.refs_18_.refs_10_), channel_id=1, source_target_pairs={{0,1},{2,3},{1,0},{4,5},{6,7},{5,4},{8,9},{10,11},{9,8},{12,13},{1... | collective-permute-start | bytes 1585160 | tf_op jit(solution)/shard_map/ppermute | solution.py:289
  6.0 3.5 %collective-permute-start.1 = (f32[1032,128]{1,0:T(8,128)S(1)}, f32[1032,128]{1,0:T(8,128)S(1)}, u32[]{:S(2)}, u32[]{:S(2)}) collective-permute-start(f32[1032,128]{1,0:T(8,128)S(1)} %pad_maximum_fusion.1.refs_12_.refs_18_.refs_10_), channel_id=1, source_target_pairs={{0,4},{1,5},{2,6},{3,7},{4,8},{5,9},{6,10},{7,11},{8,12},{9,13},{1... | collective-permute-start | bytes 1585160 | tf_op jit(solution)/shard_map/ppermute | solution.py:292
  9.5 5.0 %collective-permute-start.2 = (f32[1032,128]{1,0:T(8,128)S(1)}, f32[1032,128]{1,0:T(8,128)}, u32[]{:S(2)}, u32[]{:S(2)}) collective-permute-start(f32[1032,128]{1,0:T(8,128)S(1)} %pad_maximum_fusion.1.refs_12_.refs_18_.refs_10_), channel_id=1, source_target_pairs={{0,2},{1,3},{4,6},{5,7},{8,10},{9,11},{12,14},{13,15},{16,18},{17,... | collective-permute-start | bytes 1585160 | tf_op jit(solution)/shard_map/ppermute | solution.py:289
  14.5 4.6 %shard_map.46 = (bf16[4,512,256]{2,1,0:T(8,128)(2,1)}, bf16[4,512,256]{2,1,0:T(8,128)(2,1)}, f32[512,512]{1,0:T(8,128)}) custom-call(f32[4096,128]{1,0:T(8,128)} %bitcast.16), custom_call_target="tpu_custom_call" | custom-call | tf_op jit(solution)/shard_map/pallas_call | solution.py:82
  20.4 4.0 %collective-permute-done.2.refs_7_.refs_13_ = f32[1032,128]{1,0:T(8,128)} collective-permute-done((f32[1032,128]{1,0:T(8,128)S(1)}, f32[1032,128]{1,0:T(8,128)}, u32[]{:S(2)}, u32[]{:S(2)}) %collective-permute-start.2) | collective-permute-done | bytes 528416 | tf_op jit(solution)/shard_map/ppermute | solution.py:289
  24.6 2.7 %collective-permute-start.5 = (f32[1032,128]{1,0:T(8,128)S(1)}, f32[1032,128]{1,0:T(8,128)S(1)}, u32[]{:S(2)}, u32[]{:S(2)}) collective-permute-start(f32[1032,128]{1,0:T(8,128)S(1)} %get-tuple-element.57), channel_id=1, source_target_pairs={{0,2},{2,0},{1,3},{3,1},{4,6},{6,4},{5,7},{7,5},{8,10},{10,8},{9,1... | collective-permute-start | bytes 1585160 | tf_op jit(solution)/shard_map/ppermute | solution.py:289
  27.3 3.5 %collective-permute-start.4 = (f32[1024,128]{1,0:T(8,128)S(1)}, f32[1024,128]{1,0:T(8,128)S(1)}, u32[]{:S(2)}, u32[]{:S(2)}) collective-permute-start(f32[1024,128]{1,0:T(8,128)S(1)} %slice.33), channel_id=1, source_target_pairs={{0,4},{1,5},{2,6},{3,7},{4,8},{5,9},{6,10},{7,11},{8,12},{9,13},{1... | collective-permute-start | bytes 1572872 | tf_op jit(solution)/shard_map/ppermute | solution.py:292
  30.7 9.4 %collective-permute-done.4.refs_3_.refs_9_ = f32[1024,128]{1,0:T(8,128)S(1)} collective-permute-done((f32[1024,128]{1,0:T(8,128)S(1)}, f32[1024,128]{1,0:T(8,128)S(1)}, u32[]{:S(2)}, u32[]{:S(2)}) %collective-permute-start.4) | collective-permute-done | bytes 524320 | tf_op jit(solution)/shard_map/ppermute | solution.py:292
  42.9 4.4 %collective-permute-start.7 = (f32[1024,128]{1,0:T(8,128)S(1)}, f32[1024,128]{1,0:T(8,128)S(1)}, u32[]{:S(2)}, u32[]{:S(2)}) collective-permute-start(f32[1024,128]{1,0:T(8,128)S(1)} %get-tuple-element.56), channel_id=1, source_target_pairs={{0,4},{1,5},{2,6},{3,7},{4,8},{5,9},{6,10},{7,11},{8,12},{9,13},{1... | collective-permute-start | bytes 1572872 | tf_op jit(solution)/shard_map/ppermute | solution.py:292
  47.3 4.5 %collective-permute-start.12 = (f32[1032,128]{1,0:T(8,128)}, f32[1032,128]{1,0:T(8,128)}, u32[]{:S(2)}, u32[]{:S(2)}) collective-permute-start(f32[1032,128]{1,0:T(8,128)} %collective-permute-done.refs_2_.refs_8_), channel_id=1, source_target_pairs={{0,2},{1,3},{4,6},{5,7},{8,10},{9,11},{12,14},{13,15},{16,18},{17,... | collective-permute-start | bytes 1585160 | tf_op jit(solution)/shard_map/ppermute | solution.py:289
  52.0 2.8 %collective-permute-done.8.refs_9_.refs_15_ = f32[1024,128]{1,0:T(8,128)} collective-permute-done((f32[1024,128]{1,0:T(8,128)S(1)}, f32[1024,128]{1,0:T(8,128)}, u32[]{:S(2)}, u32[]{:S(2)}) %collective-permute-start.8) | collective-permute-done | bytes 524320 | tf_op jit(solution)/shard_map/ppermute | solution.py:289
  59.4 5.3 %collective-permute-start.10 = (f32[1024,128]{1,0:T(8,128)}, f32[1024,128]{1,0:T(8,128)}, u32[]{:S(2)}, u32[]{:S(2)}) collective-permute-start(f32[1024,128]{1,0:T(8,128)} %get-tuple-element.55), channel_id=1, source_target_pairs={{0,4},{1,5},{2,6},{3,7},{4,8},{5,9},{6,10},{7,11},{8,12},{9,13},{1... | collective-permute-start | bytes 1572872 | tf_op jit(solution)/shard_map/ppermute | solution.py:292
  66.2 7.5 %collective-permute-done.11.refs_10_.refs_16_ = f32[1024,128]{1,0:T(8,128)S(1)} collective-permute-done((f32[1024,128]{1,0:T(8,128)}, f32[1024,128]{1,0:T(8,128)S(1)}, u32[]{:S(2)}, u32[]{:S(2)}) %collective-permute-start.11) | collective-permute-done | bytes 524320 | tf_op jit(solution)/shard_map/ppermute | solution.py:289
  76.4 2.3 %maximum_select_fusion = f32[2056,128]{1,0:T(8,128)} fusion(f32[1024,128]{1,0:T(8,128)} %collective-permute-done.6.refs_4_.refs_10_, f32[1032,128]{1,0:T(8,128)S(1)} %collective-permute-done.3.refs_3_.refs_9_, f32[1024,128]{1,0:T(8,128)} %collective-permute-done.8.refs_9_.refs_15_, f32[1032,128]{1,0:T(8,128)S(1)} %collective-permute-done.5.refs_8_.refs_14_, ...), kind=kLoop, calls=%fused_computation | loop fusion | flops 789504 | bytes 3158017 | tf_op jit(solution)/shard_map/jit(_where)/select_n | solution.py:343
  78.7 4.9 %shard_map.48.refs_5_ = f32[512,512]{1,0:T(8,128)} custom-call(s32[2]{0:T(128)} %add_convert_fusion.flag_ref.refs_1_, bf16[4,512,256]{2,1,0:T(8,128)(2,1)} %get-tuple-element.49.refs_0_, bf16[4,512,256]{2,1,0:T(8,128)(2,1)} %get-tuple-element.50.refs_1_, f32[1032,128]{1,0:T(8,128)} %copy-done.4, f32[1024,128]{1,0:T(8,128)} %copy-done.5, ...), custom_call_target="tpu_custom_call" | custom-call | tf_op jit(solution)/shard_map/pallas_call | solution.py:82
  83.7 3.5 %collective-permute-start.19 = (f32[2056,128]{1,0:T(8,128)}, f32[2056,128]{1,0:T(8,128)S(1)}, u32[]{:S(2)}, u32[]{:S(2)}) collective-permute-start(f32[2056,128]{1,0:T(8,128)} %maximum_select_fusion), channel_id=1, source_target_pairs={{0,1},{1,3},{3,2},{2,0},{4,5},{5,7},{7,6},{6,4},{8,9},{9,11},{11,1... | collective-permute-start | bytes 3158024 | tf_op jit(solution)/shard_map/ppermute | solution.py:289
  88.2 6.9 %shard_map.47 = (f32[512,512]{1,0:T(8,128)}, f32[512,512]{1,0:T(8,128)}) custom-call(s32[2]{0:T(128)} %add_convert_fusion.flag_ref.refs_1_, bf16[4,512,256]{2,1,0:T(8,128)(2,1)} %get-tuple-element.49.refs_0_, bf16[4,512,256]{2,1,0:T(8,128)(2,1)} %get-tuple-element.50.refs_1_, f32[1032,128]{1,0:T(8,128)} %collective-permute-done.refs_2_.refs_8_, ...), custom_call_target="tpu_custom_call" | custom-call | tf_op jit(solution)/shard_map/pallas_call | solution.py:82
  95.7 3.1 %collective-permute-start.20 = (f32[1024,128]{1,0:T(8,128)S(1)}, f32[1024,128]{1,0:T(8,128)S(1)}, u32[]{:S(2)}, u32[]{:S(2)}) collective-permute-start(f32[1024,128]{1,0:T(8,128)S(1)} %copy-done.10), channel_id=1, source_target_pairs={{0,1},{1,0},{2,3},{3,2},{4,5},{5,4},{6,7},{7,6},{8,9},{9,8},{10,11... | collective-permute-start | bytes 1572872 | tf_op jit(solution)/shard_map/ppermute | solution.py:289
  104.9 8.7 %shard_map.49.refs_7_ = f32[4096,128]{1,0:T(8,128)} custom-call(f32[2]{0:T(128)} %pad_maximum_fusion.3.refs_0_, s32[2]{0:T(128)} %add_convert_fusion.flag_ref.refs_1_, f32[1,512]{1,0:T(1,128)} %bitcast.22, f32[512,512]{1,0:T(8,128)} %get-tuple-element.36.refs_3_, f32[512,512]{1,0:T(8,128)} %collective-permute-done.17.refs_4_, f32[512,512]{1,0:T(8,128)} %shard_map.48.refs_5_, ...), custom_call_target="tpu_custom_call" | custom-call | tf_op jit(solution)/shard_map/pallas_call | solution.py:82
  113.6 9.2 %shard_map.50.refs_5_ = f32[4096,128]{1,0:T(8,128)} custom-call(f32[2]{0:T(128)} %pad_maximum_fusion.2.refs_0_, s32[2]{0:T(128)} %add_convert_fusion.flag_ref.refs_1_, f32[1,512]{1,0:T(1,128)} %bitcast.23, f32[512,512]{1,0:T(8,128)} %get-tuple-element.44.refs_3_, f32[512,512]{1,0:T(8,128)} %collective-permute-done.15.refs_4_, ...), custom_call_target="tpu_custom_call" | custom-call | tf_op jit(solution)/shard_map/pallas_call | solution.py:82
  124.5 4.4 %shard_map.51.refs_2_ = f32[512,512]{1,0:T(8,128)} custom-call(s32[2]{0:T(128)} %add_convert_fusion.flag_ref.refs_1_, bf16[4,512,256]{2,1,0:T(8,128)(2,1)} %get-tuple-element.49.refs_0_, bf16[4,512,256]{2,1,0:T(8,128)(2,1)} %get-tuple-element.50.refs_1_, f32[1032,128]{1,0:T(8,128)} %collective-permute-done.12.refs_2_.refs_6_, f32[2056,128]{1,0:T(8,128)} %copy-done.8, ...), custom_call_target="tpu_custom_call" | custom-call | tf_op jit(solution)/shard_map/pallas_call | solution.py:82
  129.0 4.1 %collective-permute-done.21.refs_4_.refs_9_ = f32[1024,128]{1,0:T(8,128)S(1)} collective-permute-done((f32[1024,128]{1,0:T(8,128)}, f32[1024,128]{1,0:T(8,128)S(1)}, u32[]{:S(2)}, u32[]{:S(2)}) %collective-permute-start.21) | collective-permute-done | bytes 524320 | tf_op jit(solution)/shard_map/ppermute | solution.py:289
  133.8 3.6 %shard_map.52.refs_3_ = f32[512,512]{1,0:T(8,128)} custom-call(s32[2]{0:T(128)} %add_convert_fusion.flag_ref.refs_1_, bf16[4,512,256]{2,1,0:T(8,128)(2,1)} %get-tuple-element.49.refs_0_, bf16[4,512,256]{2,1,0:T(8,128)(2,1)} %get-tuple-element.50.refs_1_, f32[512,512]{1,0:T(8,128)} %shard_map.51.refs_2_, f32[1024,128]{1,0:T(8,128)} %copy-done.7, ...), custom_call_target="tpu_custom_call" | custom-call | tf_op jit(solution)/shard_map/pallas_call | solution.py:82
  141.3 6.2 %shard_map.53 = f32[4096,128]{1,0:T(8,128)} custom-call(f32[1]{0:T(128)} %bitcast.1.refs_0_, s32[2]{0:T(128)} %add_convert_fusion.flag_ref.refs_1_, f32[1,512]{1,0:T(1,128)} %bitcast.24, f32[512,512]{1,0:T(8,128)} %shard_map.52.refs_3_, f32[512,512]{1,0:T(8,128)} %copy-done.14, f32[4096,128]{1,0:T(8,128)} %shard_map.50.refs_5_, ...), custom_call_target="tpu_custom_call" | custom-call | tf_op jit(solution)/shard_map/pallas_call | solution.py:82
  (75 shorter events, 25.0 us)
Async XLA Ops:
  1.1 18.1 %collective-permute-start = (f32[1032,128]{1,0:T(8,128)S(1)}, f32[1032,128]{1,0:T(8,128)}, u32[]{:S(2)}, u32[]{:S(2)}) collective-permute-start(f32[1032,128]{1,0:T(8,128)S(1)} %pad_maximum_fusion.1.refs_12_.refs_18_.refs_10_), channel_id=1, source_target_pairs={{0,1},{2,3},{1,0},{4,5},{6,7},{5,4},{8,9},{10,11},{9,8},{12,13},{1... | collective-permute-start | bytes 1585160 | tf_op jit(solution)/shard_map/ppermute | solution.py:289
  6.0 14.5 %collective-permute-start.1 = (f32[1032,128]{1,0:T(8,128)S(1)}, f32[1032,128]{1,0:T(8,128)S(1)}, u32[]{:S(2)}, u32[]{:S(2)}) collective-permute-start(f32[1032,128]{1,0:T(8,128)S(1)} %pad_maximum_fusion.1.refs_12_.refs_18_.refs_10_), channel_id=1, source_target_pairs={{0,4},{1,5},{2,6},{3,7},{4,8},{5,9},{6,10},{7,11},{8,12},{9,13},{1... | collective-permute-start | bytes 1585160 | tf_op jit(solution)/shard_map/ppermute | solution.py:292
  9.5 14.9 %collective-permute-start.2 = (f32[1032,128]{1,0:T(8,128)S(1)}, f32[1032,128]{1,0:T(8,128)}, u32[]{:S(2)}, u32[]{:S(2)}) collective-permute-start(f32[1032,128]{1,0:T(8,128)S(1)} %pad_maximum_fusion.1.refs_12_.refs_18_.refs_10_), channel_id=1, source_target_pairs={{0,2},{1,3},{4,6},{5,7},{8,10},{9,11},{12,14},{13,15},{16,18},{17,... | collective-permute-start | bytes 1585160 | tf_op jit(solution)/shard_map/ppermute | solution.py:289
  24.5 15.6 %collective-permute-start.3 = (f32[1032,128]{1,0:T(8,128)S(1)}, f32[1032,128]{1,0:T(8,128)S(1)}, u32[]{:S(2)}, u32[]{:S(2)}) collective-permute-start(f32[1032,128]{1,0:T(8,128)S(1)} %get-tuple-element.58), channel_id=1, source_target_pairs={{0,1},{1,0},{2,3},{3,2},{4,5},{5,4},{6,7},{7,6},{8,9},{9,8},{10,11... | collective-permute-start | bytes 1585160 | tf_op jit(solution)/shard_map/ppermute | solution.py:289
  24.6 15.5 %collective-permute-start.5 = (f32[1032,128]{1,0:T(8,128)S(1)}, f32[1032,128]{1,0:T(8,128)S(1)}, u32[]{:S(2)}, u32[]{:S(2)}) collective-permute-start(f32[1032,128]{1,0:T(8,128)S(1)} %get-tuple-element.57), channel_id=1, source_target_pairs={{0,2},{2,0},{1,3},{3,1},{4,6},{6,4},{5,7},{7,5},{8,10},{10,8},{9,1... | collective-permute-start | bytes 1585160 | tf_op jit(solution)/shard_map/ppermute | solution.py:289
  27.3 12.8 %collective-permute-start.4 = (f32[1024,128]{1,0:T(8,128)S(1)}, f32[1024,128]{1,0:T(8,128)S(1)}, u32[]{:S(2)}, u32[]{:S(2)}) collective-permute-start(f32[1024,128]{1,0:T(8,128)S(1)} %slice.33), channel_id=1, source_target_pairs={{0,4},{1,5},{2,6},{3,7},{4,8},{5,9},{6,10},{7,11},{8,12},{9,13},{1... | collective-permute-start | bytes 1572872 | tf_op jit(solution)/shard_map/ppermute | solution.py:292
  40.1 36.2 %copy-start.3 = (f32[1032,128]{1,0:T(8,128)}, f32[1032,128]{1,0:T(8,128)S(1)}, u32[]{:S(2)}) copy-start(f32[1032,128]{1,0:T(8,128)S(1)} %collective-permute-done.5.refs_8_.refs_14_) | copy-start | bytes 1585156
  40.9 11.1 %collective-permute-start.6 = (f32[1024,128]{1,0:T(8,128)S(1)}, f32[1024,128]{1,0:T(8,128)}, u32[]{:S(2)}, u32[]{:S(2)}) collective-permute-start(f32[1024,128]{1,0:T(8,128)S(1)} %get-tuple-element.54), channel_id=1, source_target_pairs={{0,1},{1,0},{2,3},{3,2},{4,5},{5,4},{6,7},{7,6},{8,9},{9,8},{10,11... | collective-permute-start | bytes 1572872 | tf_op jit(solution)/shard_map/ppermute | solution.py:289
  42.6 12.2 %collective-permute-start.8 = (f32[1024,128]{1,0:T(8,128)S(1)}, f32[1024,128]{1,0:T(8,128)}, u32[]{:S(2)}, u32[]{:S(2)}) collective-permute-start(f32[1024,128]{1,0:T(8,128)S(1)} %get-tuple-element.53), channel_id=1, source_target_pairs={{0,2},{2,0},{1,3},{3,1},{4,6},{6,4},{5,7},{7,5},{8,10},{10,8},{9,1... | collective-permute-start | bytes 1572872 | tf_op jit(solution)/shard_map/ppermute | solution.py:289
  42.9 12.3 %collective-permute-start.7 = (f32[1024,128]{1,0:T(8,128)S(1)}, f32[1024,128]{1,0:T(8,128)S(1)}, u32[]{:S(2)}, u32[]{:S(2)}) collective-permute-start(f32[1024,128]{1,0:T(8,128)S(1)} %get-tuple-element.56), channel_id=1, source_target_pairs={{0,4},{1,5},{2,6},{3,7},{4,8},{5,9},{6,10},{7,11},{8,12},{9,13},{1... | collective-permute-start | bytes 1572872 | tf_op jit(solution)/shard_map/ppermute | solution.py:292
  47.3 19.0 %collective-permute-start.12 = (f32[1032,128]{1,0:T(8,128)}, f32[1032,128]{1,0:T(8,128)}, u32[]{:S(2)}, u32[]{:S(2)}) collective-permute-start(f32[1032,128]{1,0:T(8,128)} %collective-permute-done.refs_2_.refs_8_), channel_id=1, source_target_pairs={{0,2},{1,3},{4,6},{5,7},{8,10},{9,11},{12,14},{13,15},{16,18},{17,... | collective-permute-start | bytes 1585160 | tf_op jit(solution)/shard_map/ppermute | solution.py:289
  56.5 17.3 %collective-permute-start.11 = (f32[1024,128]{1,0:T(8,128)}, f32[1024,128]{1,0:T(8,128)S(1)}, u32[]{:S(2)}, u32[]{:S(2)}) collective-permute-start(f32[1024,128]{1,0:T(8,128)} %get-tuple-element.51), channel_id=1, source_target_pairs={{0,2},{2,0},{1,3},{3,1},{4,6},{6,4},{5,7},{7,5},{8,10},{10,8},{9,1... | collective-permute-start | bytes 1572872 | tf_op jit(solution)/shard_map/ppermute | solution.py:289
  58.7 15.0 %collective-permute-start.9 = (f32[1024,128]{1,0:T(8,128)}, f32[1024,128]{1,0:T(8,128)S(1)}, u32[]{:S(2)}, u32[]{:S(2)}) collective-permute-start(f32[1024,128]{1,0:T(8,128)} %get-tuple-element.52), channel_id=1, source_target_pairs={{0,1},{1,0},{2,3},{3,2},{4,5},{5,4},{6,7},{7,6},{8,9},{9,8},{10,11... | collective-permute-start | bytes 1572872 | tf_op jit(solution)/shard_map/ppermute | solution.py:289
  59.4 14.3 %collective-permute-start.10 = (f32[1024,128]{1,0:T(8,128)}, f32[1024,128]{1,0:T(8,128)}, u32[]{:S(2)}, u32[]{:S(2)}) collective-permute-start(f32[1024,128]{1,0:T(8,128)} %get-tuple-element.55), channel_id=1, source_target_pairs={{0,4},{1,5},{2,6},{3,7},{4,8},{5,9},{6,10},{7,11},{8,12},{9,13},{1... | collective-permute-start | bytes 1572872 | tf_op jit(solution)/shard_map/ppermute | solution.py:292
  64.7 30.9 %collective-permute-start.17 = (f32[512,512]{1,0:T(8,128)}, f32[512,512]{1,0:T(8,128)}, u32[]{:S(2)}, u32[]{:S(2)}) collective-permute-start(f32[512,512]{1,0:T(8,128)} %get-tuple-element.36.refs_3_), channel_id=1, source_target_pairs={{0,16},{16,0},{1,17},{17,1},{2,18},{18,2},{3,19},{19,3},{4,20},{20... | collective-permute-start | bytes 3145736 | tf_op jit(solution)/shard_map/ppermute | solution.py:296
  73.7 13.4 %collective-permute-start.13 = (f32[1024,128]{1,0:T(8,128)}, f32[1024,128]{1,0:T(8,128)}, u32[]{:S(2)}, u32[]{:S(2)}) collective-permute-start(f32[1024,128]{1,0:T(8,128)} %collective-permute-done.10.refs_5_.refs_11_), channel_id=1, source_target_pairs={{1,0},{3,2},{5,4},{7,6},{9,8},{11,10},{13,12},{15,14},{17,16},{19,... | collective-permute-start | bytes 1572872 | tf_op jit(solution)/shard_map/ppermute | solution.py:289
  75.0 12.3 %collective-permute-start.14 = (f32[1024,128]{1,0:T(8,128)}, f32[1024,128]{1,0:T(8,128)S(1)}, u32[]{:S(2)}, u32[]{:S(2)}) collective-permute-start(f32[1024,128]{1,0:T(8,128)} %collective-permute-done.10.refs_5_.refs_11_), channel_id=1, source_target_pairs={{2,0},{3,1},{6,4},{7,5},{10,8},{11,9},{14,12},{15,13},{18,16},{19,... | collective-permute-start | bytes 1572872 | tf_op jit(solution)/shard_map/ppermute | solution.py:289
  83.6 15.2 %collective-permute-start.18 = (f32[512,512]{1,0:T(8,128)}, f32[512,512]{1,0:T(8,128)}, u32[]{:S(2)}, u32[]{:S(2)}) collective-permute-start(f32[512,512]{1,0:T(8,128)} %shard_map.48.refs_5_), channel_id=1, source_target_pairs={{0,16},{16,0},{1,17},{17,1},{2,18},{18,2},{3,19},{19,3},{4,20},{20... | collective-permute-start | bytes 3145736 | tf_op jit(solution)/shard_map/ppermute | solution.py:296
  83.7 39.1 %collective-permute-start.19 = (f32[2056,128]{1,0:T(8,128)}, f32[2056,128]{1,0:T(8,128)S(1)}, u32[]{:S(2)}, u32[]{:S(2)}) collective-permute-start(f32[2056,128]{1,0:T(8,128)} %maximum_select_fusion), channel_id=1, source_target_pairs={{0,1},{1,3},{3,2},{2,0},{4,5},{5,7},{7,6},{6,4},{8,9},{9,11},{11,1... | collective-permute-start | bytes 3158024 | tf_op jit(solution)/shard_map/ppermute | solution.py:289
  95.1 18.5 %collective-permute-start.15 = (f32[512,512]{1,0:T(8,128)}, f32[512,512]{1,0:T(8,128)}, u32[]{:S(2)}, u32[]{:S(2)}) collective-permute-start(f32[512,512]{1,0:T(8,128)} %get-tuple-element.44.refs_3_), channel_id=1, source_target_pairs={{0,16},{16,0},{1,17},{17,1},{2,18},{18,2},{3,19},{19,3},{4,20},{20... | collective-permute-start | bytes 3145736 | tf_op jit(solution)/shard_map/ppermute | solution.py:296
  95.2 18.4 %collective-permute-start.16 = (f32[512,512]{1,0:T(8,128)}, f32[512,512]{1,0:T(8,128)}, u32[]{:S(2)}, u32[]{:S(2)}) collective-permute-start(f32[512,512]{1,0:T(8,128)} %get-tuple-element.45.refs_5_), channel_id=1, source_target_pairs={{0,16},{16,0},{1,17},{17,1},{2,18},{18,2},{3,19},{19,3},{4,20},{20... | collective-permute-start | bytes 3145736 | tf_op jit(solution)/shard_map/ppermute | solution.py:296
  95.7 27.1 %collective-permute-start.20 = (f32[1024,128]{1,0:T(8,128)S(1)}, f32[1024,128]{1,0:T(8,128)S(1)}, u32[]{:S(2)}, u32[]{:S(2)}) collective-permute-start(f32[1024,128]{1,0:T(8,128)S(1)} %copy-done.10), channel_id=1, source_target_pairs={{0,1},{1,0},{2,3},{3,2},{4,5},{5,4},{6,7},{7,6},{8,9},{9,8},{10,11... | collective-permute-start | bytes 1572872 | tf_op jit(solution)/shard_map/ppermute | solution.py:289
  98.8 34.3 %collective-permute-start.21 = (f32[1024,128]{1,0:T(8,128)}, f32[1024,128]{1,0:T(8,128)S(1)}, u32[]{:S(2)}, u32[]{:S(2)}) collective-permute-start(f32[1024,128]{1,0:T(8,128)} %copy-done.12), channel_id=1, source_target_pairs={{0,1},{1,0},{4,5},{5,4},{8,9},{9,8},{12,13},{13,12},{16,17},{17,16... | collective-permute-start | bytes 1572872 | tf_op jit(solution)/shard_map/ppermute | solution.py:289
  137.4 2.9 %collective-permute-start.22 = (f32[512,512]{1,0:T(8,128)}, f32[512,512]{1,0:T(8,128)S(1)}, u32[]{:S(2)}, u32[]{:S(2)}) collective-permute-start(f32[512,512]{1,0:T(8,128)} %shard_map.52.refs_3_), channel_id=1, source_target_pairs={{0,16},{16,0},{1,17},{17,1},{2,18},{18,2},{3,19},{19,3},{4,20},{20... | collective-permute-start | bytes 3145736 | tf_op jit(solution)/shard_map/ppermute | solution.py:296
  (16 other events, 115.1 us)
where the time goes:
time: 149 us; the launch traced here: 148 us
  starting transfers between devices  50.7 us (34%)
  Pallas kernels  48.5 us (33%)
  waiting for transfers between devices  32.9 us (22%)
  local copies, waits for them, and re-layouts  6.07 us (4%)
  other arithmetic  5.78 us (4%)
  between operations  3.82 us (3%)
    pallas_call x8, Pallas kernels, call(): pl.pallas_call(kernel, out_shape=outputs, in_specs=[pl.BlockSpec(memory_s...  48.5 us
    ppermute x14, starting transfers between devices, within(): lax.ppermute(block, 'occ', [(g + a, g + b) for g in planes for a, b in mo...  33.3 us
    ppermute x14, waiting for transfers between devices, within(): lax.ppermute(block, 'occ', [(g + a, g + b) for g in planes for a, b in mo...  19.7 us
    ppermute x4, starting transfers between devices, up(): lax.ppermute(block, 'occ', [(g, g + PLANE) for g in range(groups - PLANE)])  16.7 us
    ppermute x4, waiting for transfers between devices, up(): lax.ppermute(block, 'occ', [(g, g + PLANE) for g in range(groups - PLANE)])  10.9 us
    unnamed x32, local copies, waits for them, and re-layouts  5.03 us
  transfers between devices with their start and end apart: 23, of which 11 were waited for; matrix products, arithmetic and copies ran while one was open for 4% of the time, Pallas kernels for 26%

commit v1 on v0

--- a/solution.py
+++ b/solution.py
@@ -318,42 +318,32 @@
     high, low, partial_own = prepare(own, rows, width)
     turned = (high, low)
     sums_own = totals(partial_own)
-    swap_x, swap_y = [], []
-    passed = [partial_own, up_x, up_y]
+    swap_x, swap_y, swap_d = [], [], []
+    middle = (place == 1) | (place == 2)
     for at in range(CHUNKS):
-        came, mine, *_ = lax.optimization_barrier((from_z[at], own, *passed))
+        came, mine = lax.optimization_barrier((from_z[at], own))
         if at < last:
-            from_z.append(up(part(mine, at + 1)))
             up_part = part(mine, at + 1)
             if at == 0:
                 up_part = jnp.concatenate([up_part, energies])
-            swap_x.append(within(jnp.where(odd_x, came, up_part), [(0, 1), (1, 0), (2, 3), (3, 2)]))
-            swap_y.append(within(jnp.where(odd_y, came, up_part), [(0, 2), (2, 0), (1, 3), (3, 1)]))
+            send_x, send_y = jnp.where(odd_x, came, up_part), jnp.where(odd_y, came, up_part)
+            moves_x, moves_y = [(0, 1), (1, 0), (2, 3), (3, 2)], [(0, 2), (2, 0), (1, 3), (3, 1)]
+            from_z.append(up(part(after(own, from_z[at], partial_own), at + 1)))
         else:
-            swap_x.append(within(came, [(1, 0), (3, 2)]))
-            swap_y.append(within(came, [(2, 0), (3, 1)]))
-        passed = [swap_x[at], swap_y[at]]
+            send_x, send_y = came, came
+            moves_x, moves_y = [(1, 0), (3, 2)], [(2, 0), (3, 1)]
+        swap_x.append(within(after(send_x, swap_x[at - 1] if at else (partial_own, up_x)), moves_x))
+        swap_y.append(within(after(send_y, swap_y[at - 1] if at else up_y), moves_y))
         if at == 0:
             up_d = within(up_x, [(0, 2), (1, 3)])
-        if at == 2:
-            passed.append(up_d)
-
-    middle = (place == 1) | (place == 2)
-    half = CHUNKS // 2
-    block = jnp.where(middle, jnp.concatenate(swap_x[:half]), jnp.concatenate(swap_y[:half]))
-    block = after(block, swap_x[half], swap_y[half])
-    cycle = within(block, [(0, 1), (1, 3), (3, 2), (2, 0)])
-    swap_d = [(cycle, 0)] + [(cycle, at * cut + SUBLANES) for at in range(1, half)]
-    for at in range(half, CHUNKS):
-        moves = [(0, 1), (1, 0), (2, 3), (3, 2)] if at < last else [(0, 1), (1, 0)]
-        swap_d.append((within(swap_y[at], moves), 0))
+            send_d, moves_d = jnp.where(middle, swap_x[0], swap_y[0]), [(0, 1), (1, 3), (3, 2), (2, 0)]
+        else:
+            send_d, moves_d = after(swap_y[at], swap_d[at - 1]), moves_x if at < last else [(0, 1), (1, 0)]
+        swap_d.append(within(send_d, moves_d))
 
     def pieces_of(first, swaps, flag, base):
-        places = [(array, start + base) for array, start in [(first, 0), *swaps]]
+        places = [(array, base) for array in [first, *swaps]]
         return [Piece((places[at], places[at + 1]), flag) for at in range(CHUNKS)]
-
-    swap_x = [(block, 0) for block in swap_x]
-    swap_y = [(block, 0) for block in swap_y]
 
     def whole(array, base):
         return Piece(((array, base),))
@@ -367,20 +357,23 @@
     eps_y = pieces_of(up_y, swap_y, 1, cut)[0]
     eps_d = pieces_of(up_d, swap_d, 1, cut)[0]
 
-    (partial_z,) = integrate(after(turned, block), [slot_z], [0], flags, size, width)
+    partial_z, partial_y = integrate(
+        after(turned, swap_x[2]), [slot_z, slot_y], [0, 0], flags, size, width
+    )
+    own_eps = whole(first_sent, cut)
     gradient = add(
-        [sums_own, totals(partial_z)], [slot_own, slot_z], [sign_own, sign_z],
-        [whole(first_sent, cut), whole(first_sent, cut), whole(from_z[0], cut)],
-    )
-    partial_x, partial_y = integrate(turned, [slot_x, slot_y], [0, 0], flags, size, width)
+        [sums_own, totals(partial_z), totals(partial_y)], [slot_own, slot_z, slot_y],
+        [sign_own, sign_z, sign_y], [own_eps, own_eps, whole(from_z[0], cut), eps_y],
+    )
+    turned = after(turned, gradient)
+    early = integrate(turned, [slot_x[:last], slot_d[: last - 1]], [0, 0], flags, size, width)
+    partial_x, partial_d = integrate(
+        turned, [slot_x[last:], slot_d[last - 1 : last]], [last, last - 1], flags, size, width, early
+    )
+    (partial_d,) = integrate(turned, [slot_d[last:]], [last], flags, size, width, [partial_d])
     gradient = add(
-        [totals(partial_x), totals(partial_y)], [slot_x, slot_y], [sign_x, sign_y],
-        [whole(first_sent, cut), eps_x, eps_y], gradient,
-    )
-    turned = after(turned, gradient)
-    partial_d = integrate(turned, [slot_d[:last]], [0], flags, size, width)
-    (partial_d,) = integrate(turned, [slot_d[last:]], [last], flags, size, width, partial_d)
-    gradient = add([totals(partial_d)], [slot_d], [sign_d], [whole(first_sent, cut), eps_d], gradient)
+        [totals(partial_x), totals(partial_d)], [slot_x, slot_d], [sign_x, sign_d], [own_eps, eps_x, eps_d], gradient
+    )
     return gradient.reshape(rows, occ_rows, virt)
 
 

time: 149 us -> 160 us (1.074)
  waiting for transfers between devices: 32.9 us -> 55.6 us
  starting transfers between devices: 50.7 us -> 43.6 us
  Pallas kernels: 48.5 us -> 45.7 us
  other arithmetic: 5.78 us -> 4.18 us
    ppermute x14 -> x15, waiting for transfers between devices: 19.7 us -> 39.6 us  [within(): lax.ppermute(block, 'occ', [(g + a, g + b) for g in planes for a, b in mo...]
    ppermute x14 -> x15, starting transfers between devices: 33.3 us -> 24.3 us  [within(): lax.ppermute(block, 'occ', [(g + a, g + b) for g in planes for a, b in mo...]
    ppermute x4, waiting for transfers between devices: 10.9 us -> 15.3 us  [up(): lax.ppermute(block, 'occ', [(g, g + PLANE) for g in range(groups - PLANE)])]
    pallas_call x8 -> x7, Pallas kernels: 48.5 us -> 45.7 us  [call(): pl.pallas_call(kernel, out_shape=outputs, in_specs=[pl.BlockSpec(memory_s...]
    select_n x1, other arithmetic: 2.3 us -> 0.06 us  [on_device(): jnp.where(middle, swap_x[0], swap_y[0])]
    slice x3 -> x5, local copies, waits for them, and re-layouts: 0.37 us -> 2.57 us  [part(): return whole[at * cut:(at + 1) * cut]]
    unnamed x32 -> x40, local copies, waits for them, and re-layouts: 5.03 us -> 3.85 us
  transfers between devices with their start and end apart: 23 -> 24, of which waited for: 11 -> 8; matrix products, arithmetic and copies ran while one was open for 4% -> 4% of each run, Pallas kernels for 26% -> 23%
where the time goes in v1:
time: 160 us
  waiting for transfers between devices  55.6 us (35%)
  Pallas kernels  45.7 us (29%)
  starting transfers between devices  43.6 us (27%)
  local copies, waits for them, and re-layouts  7.07 us (4%)
  other arithmetic  4.18 us (3%)
  between operations  3.75 us (2%)
    pallas_call x7, Pallas kernels, call(): pl.pallas_call(kernel, out_shape=outputs, in_specs=[pl.BlockSpec(memory_s...  45.7 us
    ppermute x15, waiting for transfers between devices, within(): lax.ppermute(block, 'occ', [(g + a, g + b) for g in planes for a, b in mo...  39.6 us
    ppermute x15, starting transfers between devices, within(): lax.ppermute(block, 'occ', [(g + a, g + b) for g in planes for a, b in mo...  24.3 us
    ppermute x4, starting transfers between devices, up(): lax.ppermute(block, 'occ', [(g, g + PLANE) for g in range(groups - PLANE)])  18 us
    ppermute x4, waiting for transfers between devices, up(): lax.ppermute(block, 'occ', [(g, g + PLANE) for g in range(groups - PLANE)])  15.3 us
    unnamed x40, local copies, waits for them, and re-layouts  3.85 us
  transfers between devices with their start and end apart: 24, of which 8 were waited for; matrix products, arithmetic and copies ran while one was open for 4% of the time, Pallas kernels for 23%

profile of v1, /device:TPU:0, one launch (start us, length us, event | category | flops | bytes accessed | tf_op | source)
XLA Modules:
  0.0 159.9 jit_solution(7274545528697102947)
XLA Ops:
  0.7 1.6 slice.37
  2.3 5.0 %collective-permute-start.1 = (f32[1032,128]{1,0:T(8,128)S(1)}, f32[1032,128]{1,0:T(8,128)S(1)}, u32[]{:S(2)}, u32[]{:S(2)}) collective-permute-start(f32[1032,128]{1,0:T(8,128)S(1)} %pad_maximum_fusion.1.refs_19_.refs_18_), channel_id=1, source_target_pairs={{0,4},{1,5},{2,6},{3,7},{4,8},{5,9},{6,10},{7,11},{8,12},{9,13},{1... | collective-permute-start | bytes 1585160 | tf_op jit(solution)/shard_map/ppermute | solution.py:292
  7.3 3.4 %collective-permute-start.4 = (f32[1032,128]{1,0:T(8,128)S(1)}, f32[1032,128]{1,0:T(8,128)}, u32[]{:S(2)}, u32[]{:S(2)}) collective-permute-start(f32[1032,128]{1,0:T(8,128)S(1)} %pad_maximum_fusion.1.refs_19_.refs_18_), channel_id=1, source_target_pairs={{0,1},{2,3},{1,0},{4,5},{6,7},{5,4},{8,9},{10,11},{9,8},{12,13},{1... | collective-permute-start | bytes 1585160 | tf_op jit(solution)/shard_map/ppermute | solution.py:289
  10.7 5.0 %collective-permute-start.9 = (f32[1032,128]{1,0:T(8,128)S(1)}, f32[1032,128]{1,0:T(8,128)}, u32[]{:S(2)}, u32[]{:S(2)}) collective-permute-start(f32[1032,128]{1,0:T(8,128)S(1)} %pad_maximum_fusion.1.refs_19_.refs_18_), channel_id=1, source_target_pairs={{0,2},{1,3},{4,6},{5,7},{8,10},{9,11},{12,14},{13,15},{16,18},{17,... | collective-permute-start | bytes 1585160 | tf_op jit(solution)/shard_map/ppermute | solution.py:289
  15.7 4.5 %shard_map.46 = (bf16[4,512,256]{2,1,0:T(8,128)(2,1)}, bf16[4,512,256]{2,1,0:T(8,128)(2,1)}, f32[512,512]{1,0:T(8,128)}) custom-call(f32[4096,128]{1,0:T(8,128)} %bitcast.16), custom_call_target="tpu_custom_call" | custom-call | tf_op jit(solution)/shard_map/pallas_call | solution.py:82
  21.2 4.2 %collective-permute-start.2 = (f32[1024,128]{1,0:T(8,128)}, f32[1024,128]{1,0:T(8,128)}, u32[]{:S(2)}, u32[]{:S(2)}) collective-permute-start(f32[1024,128]{1,0:T(8,128)} %slice.39), channel_id=1, source_target_pairs={{0,4},{1,5},{2,6},{3,7},{4,8},{5,9},{6,10},{7,11},{8,12},{9,13},{1... | collective-permute-start | bytes 1572872 | tf_op jit(solution)/shard_map/ppermute | solution.py:292
  27.1 1.5 collective-permute-start.10
  28.7 6.6 %collective-permute-done.2.refs_3_.refs_11_ = f32[1024,128]{1,0:T(8,128)} collective-permute-done((f32[1024,128]{1,0:T(8,128)}, f32[1024,128]{1,0:T(8,128)}, u32[]{:S(2)}, u32[]{:S(2)}) %collective-permute-start.2) | collective-permute-done | bytes 524320 | tf_op jit(solution)/shard_map/ppermute | solution.py:292
  35.3 4.4 %collective-permute-start.3 = (f32[1024,128]{1,0:T(8,128)S(1)}, f32[1024,128]{1,0:T(8,128)S(1)}, u32[]{:S(2)}, u32[]{:S(2)}) collective-permute-start(f32[1024,128]{1,0:T(8,128)S(1)} %slice.40), channel_id=1, source_target_pairs={{0,4},{1,5},{2,6},{3,7},{4,8},{5,9},{6,10},{7,11},{8,12},{9,13},{1... | collective-permute-start | bytes 1572872 | tf_op jit(solution)/shard_map/ppermute | solution.py:292
  43.8 5.3 %collective-permute-done.3.refs_4_.refs_12_ = f32[1024,128]{1,0:T(8,128)S(1)} collective-permute-done((f32[1024,128]{1,0:T(8,128)S(1)}, f32[1024,128]{1,0:T(8,128)S(1)}, u32[]{:S(2)}, u32[]{:S(2)}) %collective-permute-start.3) | collective-permute-done | bytes 524320 | tf_op jit(solution)/shard_map/ppermute | solution.py:292
  49.1 4.4 %collective-permute-start.8 = (f32[1024,128]{1,0:T(8,128)S(1)}, f32[1024,128]{1,0:T(8,128)S(1)}, u32[]{:S(2)}, u32[]{:S(2)}) collective-permute-start(f32[1024,128]{1,0:T(8,128)S(1)} %slice.44), channel_id=1, source_target_pairs={{0,4},{1,5},{2,6},{3,7},{4,8},{5,9},{6,10},{7,11},{8,12},{9,13},{1... | collective-permute-start | bytes 1572872 | tf_op jit(solution)/shard_map/ppermute | solution.py:292
  53.7 2.9 %collective-permute-done.11.refs_8_.refs_16_ = f32[1024,128]{1,0:T(8,128)} collective-permute-done((f32[1024,128]{1,0:T(8,128)S(1)}, f32[1024,128]{1,0:T(8,128)}, u32[]{:S(2)}, u32[]{:S(2)}) %collective-permute-start.11) | collective-permute-done | bytes 524320 | tf_op jit(solution)/shard_map/ppermute | solution.py:289
  56.6 2.0 %collective-permute-start.7 = (f32[1024,128]{1,0:T(8,128)S(1)}, f32[1024,128]{1,0:T(8,128)S(1)}, u32[]{:S(2)}, u32[]{:S(2)}) collective-permute-start(f32[1024,128]{1,0:T(8,128)S(1)} %get-tuple-element.64), channel_id=1, source_target_pairs={{0,1},{1,0},{2,3},{3,2},{4,5},{5,4},{6,7},{7,6},{8,9},{9,8},{10,11... | collective-permute-start | bytes 1572872 | tf_op jit(solution)/shard_map/ppermute | solution.py:289
  58.7 3.4 %collective-permute-done.8.refs_5_.refs_13_ = f32[1024,128]{1,0:T(8,128)S(1)} collective-permute-done((f32[1024,128]{1,0:T(8,128)S(1)}, f32[1024,128]{1,0:T(8,128)S(1)}, u32[]{:S(2)}, u32[]{:S(2)}) %collective-permute-start.8) | collective-permute-done | bytes 524320 | tf_op jit(solution)/shard_map/ppermute | solution.py:292
  62.1 13.5 %collective-permute-done.12.refs_9_.refs_17_ = f32[1024,128]{1,0:T(8,128)S(1)} collective-permute-done((f32[1024,128]{1,0:T(8,128)S(1)}, f32[1024,128]{1,0:T(8,128)S(1)}, u32[]{:S(2)}, u32[]{:S(2)}) %collective-permute-start.12) | collective-permute-done | bytes 524320 | tf_op jit(solution)/shard_map/ppermute | solution.py:289
  77.7 10.4 %collective-permute-done.13.refs_10_.refs_18_ = f32[1024,128]{1,0:T(8,128)} collective-permute-done((f32[1024,128]{1,0:T(8,128)S(1)}, f32[1024,128]{1,0:T(8,128)}, u32[]{:S(2)}, u32[]{:S(2)}) %collective-permute-start.13) | collective-permute-done | bytes 524320 | tf_op jit(solution)/shard_map/ppermute | solution.py:289
  88.1 7.1 %shard_map.47 = (f32[512,512]{1,0:T(8,128)}, f32[512,512]{1,0:T(8,128)}) custom-call(s32[2]{0:T(128)} %add_convert_fusion.flag_ref.refs_1_, bf16[4,512,256]{2,1,0:T(8,128)(2,1)} %get-tuple-element.75.refs_0_, bf16[4,512,256]{2,1,0:T(8,128)(2,1)} %get-tuple-element.76.refs_1_, f32[1032,128]{1,0:T(8,128)} %copy-done.4, ...), custom_call_target="tpu_custom_call" | custom-call | tf_op jit(solution)/shard_map/pallas_call | solution.py:82
  97.2 12.7 %collective-permute-done.20.refs_7_.refs_3_.refs_16_ = f32[1024,128]{1,0:T(8,128)S(1)} collective-permute-done((f32[1024,128]{1,0:T(8,128)}, f32[1024,128]{1,0:T(8,128)S(1)}, u32[]{:S(2)}, u32[]{:S(2)}) %collective-permute-start.20) | collective-permute-done | bytes 524320 | tf_op jit(solution)/shard_map/ppermute | solution.py:289
  111.2 4.8 %collective-permute-start.22 = (f32[1024,128]{1,0:T(8,128)}, f32[1024,128]{1,0:T(8,128)S(1)}, u32[]{:S(2)}, u32[]{:S(2)}) collective-permute-start(f32[1024,128]{1,0:T(8,128)} %collective-permute-done.13.refs_10_.refs_18_), channel_id=1, source_target_pairs={{0,1},{1,0},{4,5},{5,4},{8,9},{9,8},{12,13},{13,12},{16,17},{17,16... | collective-permute-start | bytes 1572872 | tf_op jit(solution)/shard_map/ppermute | solution.py:289
  118.6 11.3 %shard_map.48.refs_7_ = f32[4096,128]{1,0:T(8,128)} custom-call(f32[3]{0:T(128)} %pad_maximum_fusion.3.refs_0_, s32[2]{0:T(128)} %add_convert_fusion.flag_ref.refs_1_, f32[1,512]{1,0:T(1,128)} %bitcast.25, f32[512,512]{1,0:T(8,128)} %get-tuple-element.53.refs_3_, f32[512,512]{1,0:T(8,128)} %collective-permute-done.refs_4_, ...), custom_call_target="tpu_custom_call" | custom-call | tf_op jit(solution)/shard_map/pallas_call | solution.py:82
  130.7 5.5 %shard_map.49 = (f32[512,512]{1,0:T(8,128)}, f32[512,512]{1,0:T(8,128)}) custom-call(s32[2]{0:T(128)} %add_convert_fusion.flag_ref.refs_1_, bf16[4,512,256]{2,1,0:T(8,128)(2,1)} %get-tuple-element.75.refs_0_, bf16[4,512,256]{2,1,0:T(8,128)(2,1)} %get-tuple-element.76.refs_1_, f32[1032,128]{1,0:T(8,128)} %collective-permute-done.4.refs_2_.refs_8_, ...), custom_call_target="tpu_custom_call" | custom-call | tf_op jit(solution)/shard_map/pallas_call | solution.py:82
  137.1 4.6 %shard_map.50 = (f32[512,512]{1,0:T(8,128)}, f32[512,512]{1,0:T(8,128)}) custom-call(s32[2]{0:T(128)} %add_convert_fusion.flag_ref.refs_1_, bf16[4,512,256]{2,1,0:T(8,128)(2,1)} %get-tuple-element.75.refs_0_, bf16[4,512,256]{2,1,0:T(8,128)(2,1)} %get-tuple-element.76.refs_1_, f32[512,512]{1,0:T(8,128)} %get-tuple-element.78.refs_2_, ...), custom_call_target="tpu_custom_call" | custom-call | tf_op jit(solution)/shard_map/pallas_call | solution.py:82
  142.6 3.6 %shard_map.51.refs_5_ = f32[512,512]{1,0:T(8,128)} custom-call(s32[2]{0:T(128)} %add_convert_fusion.flag_ref.refs_1_, bf16[4,512,256]{2,1,0:T(8,128)(2,1)} %get-tuple-element.75.refs_0_, bf16[4,512,256]{2,1,0:T(8,128)(2,1)} %get-tuple-element.76.refs_1_, f32[512,512]{1,0:T(8,128)} %get-tuple-element.83.refs_2_, f32[1024,128]{1,0:T(8,128)} %copy-done.7, ...), custom_call_target="tpu_custom_call" | custom-call | tf_op jit(solution)/shard_map/pallas_call | solution.py:82
  150.6 9.1 %shard_map.52 = f32[4096,128]{1,0:T(8,128)} custom-call(f32[2]{0:T(128)} %pad_maximum_fusion.2.refs_0_, s32[2]{0:T(128)} %add_convert_fusion.flag_ref.refs_1_, f32[1,512]{1,0:T(1,128)} %bitcast.26, f32[512,512]{1,0:T(8,128)} %get-tuple-element.82.refs_3_, f32[512,512]{1,0:T(8,128)} %copy-done.17, f32[512,512]{1,0:T(8,128)} %shard_map.51.refs_5_, ...), custom_call_target="tpu_custom_call" | custom-call | tf_op jit(solution)/shard_map/pallas_call | solution.py:82
  (86 shorter events, 19.2 us)
Async XLA Ops:
  2.3 17.9 %collective-permute-start.1 = (f32[1032,128]{1,0:T(8,128)S(1)}, f32[1032,128]{1,0:T(8,128)S(1)}, u32[]{:S(2)}, u32[]{:S(2)}) collective-permute-start(f32[1032,128]{1,0:T(8,128)S(1)} %pad_maximum_fusion.1.refs_19_.refs_18_), channel_id=1, source_target_pairs={{0,4},{1,5},{2,6},{3,7},{4,8},{5,9},{6,10},{7,11},{8,12},{9,13},{1... | collective-permute-start | bytes 1585160 | tf_op jit(solution)/shard_map/ppermute | solution.py:292
  7.3 19.3 %collective-permute-start.4 = (f32[1032,128]{1,0:T(8,128)S(1)}, f32[1032,128]{1,0:T(8,128)}, u32[]{:S(2)}, u32[]{:S(2)}) collective-permute-start(f32[1032,128]{1,0:T(8,128)S(1)} %pad_maximum_fusion.1.refs_19_.refs_18_), channel_id=1, source_target_pairs={{0,1},{2,3},{1,0},{4,5},{6,7},{5,4},{8,9},{10,11},{9,8},{12,13},{1... | collective-permute-start | bytes 1585160 | tf_op jit(solution)/shard_map/ppermute | solution.py:289
  10.7 16.5 %collective-permute-start.9 = (f32[1032,128]{1,0:T(8,128)S(1)}, f32[1032,128]{1,0:T(8,128)}, u32[]{:S(2)}, u32[]{:S(2)}) collective-permute-start(f32[1032,128]{1,0:T(8,128)S(1)} %pad_maximum_fusion.1.refs_19_.refs_18_), channel_id=1, source_target_pairs={{0,2},{1,3},{4,6},{5,7},{8,10},{9,11},{12,14},{13,15},{16,18},{17,... | collective-permute-start | bytes 1585160 | tf_op jit(solution)/shard_map/ppermute | solution.py:289
  21.2 14.1 %collective-permute-start.2 = (f32[1024,128]{1,0:T(8,128)}, f32[1024,128]{1,0:T(8,128)}, u32[]{:S(2)}, u32[]{:S(2)}) collective-permute-start(f32[1024,128]{1,0:T(8,128)} %slice.39), channel_id=1, source_target_pairs={{0,4},{1,5},{2,6},{3,7},{4,8},{5,9},{6,10},{7,11},{8,12},{9,13},{1... | collective-permute-start | bytes 1572872 | tf_op jit(solution)/shard_map/ppermute | solution.py:292
  26.5 14.3 %collective-permute-start.5 = (f32[1032,128]{1,0:T(8,128)}, f32[1032,128]{1,0:T(8,128)S(1)}, u32[]{:S(2)}, u32[]{:S(2)}) collective-permute-start(f32[1032,128]{1,0:T(8,128)} %get-tuple-element.62), channel_id=1, source_target_pairs={{0,1},{1,0},{2,3},{3,2},{4,5},{5,4},{6,7},{7,6},{8,9},{9,8},{10,11... | collective-permute-start | bytes 1585160 | tf_op jit(solution)/shard_map/ppermute | solution.py:289
  27.1 14.5 %collective-permute-start.10 = (f32[1032,128]{1,0:T(8,128)}, f32[1032,128]{1,0:T(8,128)S(1)}, u32[]{:S(2)}, u32[]{:S(2)}) collective-permute-start(f32[1032,128]{1,0:T(8,128)} %get-tuple-element.68), channel_id=1, source_target_pairs={{0,2},{2,0},{1,3},{3,1},{4,6},{6,4},{5,7},{7,5},{8,10},{10,8},{9,1... | collective-permute-start | bytes 1585160 | tf_op jit(solution)/shard_map/ppermute | solution.py:289
  35.3 13.8 %collective-permute-start.3 = (f32[1024,128]{1,0:T(8,128)S(1)}, f32[1024,128]{1,0:T(8,128)S(1)}, u32[]{:S(2)}, u32[]{:S(2)}) collective-permute-start(f32[1024,128]{1,0:T(8,128)S(1)} %slice.40), channel_id=1, source_target_pairs={{0,4},{1,5},{2,6},{3,7},{4,8},{5,9},{6,10},{7,11},{8,12},{9,13},{1... | collective-permute-start | bytes 1572872 | tf_op jit(solution)/shard_map/ppermute | solution.py:292
  40.9 15.7 %collective-permute-start.6 = (f32[1024,128]{1,0:T(8,128)S(1)}, f32[1024,128]{1,0:T(8,128)S(1)}, u32[]{:S(2)}, u32[]{:S(2)}) collective-permute-start(f32[1024,128]{1,0:T(8,128)S(1)} %get-tuple-element.63), channel_id=1, source_target_pairs={{0,1},{1,0},{2,3},{3,2},{4,5},{5,4},{6,7},{7,6},{8,9},{9,8},{10,11... | collective-permute-start | bytes 1572872 | tf_op jit(solution)/shard_map/ppermute | solution.py:289
  41.6 15.0 %collective-permute-start.11 = (f32[1024,128]{1,0:T(8,128)S(1)}, f32[1024,128]{1,0:T(8,128)}, u32[]{:S(2)}, u32[]{:S(2)}) collective-permute-start(f32[1024,128]{1,0:T(8,128)S(1)} %get-tuple-element.69), channel_id=1, source_target_pairs={{0,2},{2,0},{1,3},{3,1},{4,6},{6,4},{5,7},{7,5},{8,10},{10,8},{9,1... | collective-permute-start | bytes 1572872 | tf_op jit(solution)/shard_map/ppermute | solution.py:289
  43.2 33.7 %collective-permute-start.17 = (f32[1032,128]{1,0:T(8,128)S(1)}, f32[1032,128]{1,0:T(8,128)S(1)}, u32[]{:S(2)}, u32[]{:S(2)}) collective-permute-start(f32[1032,128]{1,0:T(8,128)S(1)} %broadcast_select_fusion), channel_id=1, source_target_pairs={{0,1},{1,3},{3,2},{2,0},{4,5},{5,7},{7,6},{6,4},{8,9},{9,11},{11,1... | collective-permute-start | bytes 1585160 | tf_op jit(solution)/shard_map/ppermute | solution.py:289
  49.1 13.0 %collective-permute-start.8 = (f32[1024,128]{1,0:T(8,128)S(1)}, f32[1024,128]{1,0:T(8,128)S(1)}, u32[]{:S(2)}, u32[]{:S(2)}) collective-permute-start(f32[1024,128]{1,0:T(8,128)S(1)} %slice.44), channel_id=1, source_target_pairs={{0,4},{1,5},{2,6},{3,7},{4,8},{5,9},{6,10},{7,11},{8,12},{9,13},{1... | collective-permute-start | bytes 1572872 | tf_op jit(solution)/shard_map/ppermute | solution.py:292
  56.6 19.0 %collective-permute-start.12 = (f32[1024,128]{1,0:T(8,128)S(1)}, f32[1024,128]{1,0:T(8,128)S(1)}, u32[]{:S(2)}, u32[]{:S(2)}) collective-permute-start(f32[1024,128]{1,0:T(8,128)S(1)} %get-tuple-element.70), channel_id=1, source_target_pairs={{0,2},{2,0},{1,3},{3,1},{4,6},{6,4},{5,7},{7,5},{8,10},{10,8},{9,1... | collective-permute-start | bytes 1572872 | tf_op jit(solution)/shard_map/ppermute | solution.py:289
  56.6 21.1 %collective-permute-start.7 = (f32[1024,128]{1,0:T(8,128)S(1)}, f32[1024,128]{1,0:T(8,128)S(1)}, u32[]{:S(2)}, u32[]{:S(2)}) collective-permute-start(f32[1024,128]{1,0:T(8,128)S(1)} %get-tuple-element.64), channel_id=1, source_target_pairs={{0,1},{1,0},{2,3},{3,2},{4,5},{5,4},{6,7},{7,6},{8,9},{9,8},{10,11... | collective-permute-start | bytes 1572872 | tf_op jit(solution)/shard_map/ppermute | solution.py:289
  75.6 12.5 %collective-permute-start.13 = (f32[1024,128]{1,0:T(8,128)S(1)}, f32[1024,128]{1,0:T(8,128)}, u32[]{:S(2)}, u32[]{:S(2)}) collective-permute-start(f32[1024,128]{1,0:T(8,128)S(1)} %collective-permute-done.8.refs_5_.refs_13_), channel_id=1, source_target_pairs={{2,0},{3,1},{6,4},{7,5},{10,8},{11,9},{14,12},{15,13},{18,16},{19,... | collective-permute-start | bytes 1572872 | tf_op jit(solution)/shard_map/ppermute | solution.py:289
  76.9 18.9 %collective-permute-start.18 = (f32[1024,128]{1,0:T(8,128)}, f32[1024,128]{1,0:T(8,128)S(1)}, u32[]{:S(2)}, u32[]{:S(2)}) collective-permute-start(f32[1024,128]{1,0:T(8,128)} %collective-permute-done.11.refs_8_.refs_16_), channel_id=1, source_target_pairs={{0,1},{1,0},{2,3},{3,2},{4,5},{5,4},{6,7},{7,6},{8,9},{9,8},{10,11... | collective-permute-start | bytes 1572872 | tf_op jit(solution)/shard_map/ppermute | solution.py:289
  77.0 34.2 %collective-permute-start = (f32[512,512]{1,0:T(8,128)}, f32[512,512]{1,0:T(8,128)}, u32[]{:S(2)}, u32[]{:S(2)}) collective-permute-start(f32[512,512]{1,0:T(8,128)} %get-tuple-element.53.refs_3_), channel_id=1, source_target_pairs={{0,16},{16,0},{1,17},{17,1},{2,18},{18,2},{3,19},{19,3},{4,20},{20... | collective-permute-start | bytes 3145736 | tf_op jit(solution)/shard_map/ppermute | solution.py:296
  95.2 23.4 %collective-permute-start.14 = (f32[512,512]{1,0:T(8,128)}, f32[512,512]{1,0:T(8,128)}, u32[]{:S(2)}, u32[]{:S(2)}) collective-permute-start(f32[512,512]{1,0:T(8,128)} %get-tuple-element.73.refs_5_), channel_id=1, source_target_pairs={{0,16},{16,0},{1,17},{17,1},{2,18},{18,2},{3,19},{19,3},{4,20},{20... | collective-permute-start | bytes 3145736 | tf_op jit(solution)/shard_map/ppermute | solution.py:296
  95.3 23.3 %collective-permute-start.15 = (f32[512,512]{1,0:T(8,128)}, f32[512,512]{1,0:T(8,128)}, u32[]{:S(2)}, u32[]{:S(2)}) collective-permute-start(f32[512,512]{1,0:T(8,128)} %get-tuple-element.74.refs_7_), channel_id=1, source_target_pairs={{0,16},{16,0},{1,17},{17,1},{2,18},{18,2},{3,19},{19,3},{4,20},{20... | collective-permute-start | bytes 3145736 | tf_op jit(solution)/shard_map/ppermute | solution.py:296
  95.8 14.1 %collective-permute-start.20 = (f32[1024,128]{1,0:T(8,128)}, f32[1024,128]{1,0:T(8,128)S(1)}, u32[]{:S(2)}, u32[]{:S(2)}) collective-permute-start(f32[1024,128]{1,0:T(8,128)} %copy-done.16), channel_id=1, source_target_pairs={{0,1},{1,0},{2,3},{3,2},{4,5},{5,4},{6,7},{7,6},{8,9},{9,8},{10,11... | collective-permute-start | bytes 1572872 | tf_op jit(solution)/shard_map/ppermute | solution.py:289
  95.8 34.1 %collective-permute-start.16 = (f32[1032,128]{1,0:T(8,128)}, f32[1032,128]{1,0:T(8,128)S(1)}, u32[]{:S(2)}, u32[]{:S(2)}) collective-permute-start(f32[1032,128]{1,0:T(8,128)} %collective-permute-done.4.refs_2_.refs_8_), channel_id=1, source_target_pairs={{0,2},{1,3},{4,6},{5,7},{8,10},{9,11},{12,14},{13,15},{16,18},{17,... | collective-permute-start | bytes 1585160 | tf_op jit(solution)/shard_map/ppermute | solution.py:289
  109.9 26.3 %collective-permute-start.19 = (f32[1024,128]{1,0:T(8,128)S(1)}, f32[1024,128]{1,0:T(8,128)S(1)}, u32[]{:S(2)}, u32[]{:S(2)}) collective-permute-start(f32[1024,128]{1,0:T(8,128)S(1)} %copy-done.15), channel_id=1, source_target_pairs={{1,0},{3,2},{5,4},{7,6},{9,8},{11,10},{13,12},{15,14},{17,16},{19,... | collective-permute-start | bytes 1572872 | tf_op jit(solution)/shard_map/ppermute | solution.py:289
  111.2 30.6 %collective-permute-start.22 = (f32[1024,128]{1,0:T(8,128)}, f32[1024,128]{1,0:T(8,128)S(1)}, u32[]{:S(2)}, u32[]{:S(2)}) collective-permute-start(f32[1024,128]{1,0:T(8,128)} %collective-permute-done.13.refs_10_.refs_18_), channel_id=1, source_target_pairs={{0,1},{1,0},{4,5},{5,4},{8,9},{9,8},{12,13},{13,12},{16,17},{17,16... | collective-permute-start | bytes 1572872 | tf_op jit(solution)/shard_map/ppermute | solution.py:289
  141.7 6.9 %collective-permute-start.21 = (f32[512,512]{1,0:T(8,128)}, f32[512,512]{1,0:T(8,128)S(1)}, u32[]{:S(2)}, u32[]{:S(2)}) collective-permute-start(f32[512,512]{1,0:T(8,128)} %get-tuple-element.82.refs_3_), channel_id=1, source_target_pairs={{0,16},{16,0},{1,17},{17,1},{2,18},{18,2},{3,19},{19,3},{4,20},{20... | collective-permute-start | bytes 3145736 | tf_op jit(solution)/shard_map/ppermute | solution.py:296
  146.2 3.1 %collective-permute-start.23 = (f32[512,512]{1,0:T(8,128)}, f32[512,512]{1,0:T(8,128)S(1)}, u32[]{:S(2)}, u32[]{:S(2)}) collective-permute-start(f32[512,512]{1,0:T(8,128)} %shard_map.51.refs_5_), channel_id=1, source_target_pairs={{0,16},{16,0},{1,17},{17,1},{2,18},{18,2},{3,19},{19,3},{4,20},{20... | collective-permute-start | bytes 3145736 | tf_op jit(solution)/shard_map/ppermute | solution.py:296
  (20 other events, 299.0 us)
